TPU v7x, 32 devices: a whole 2x2x4 slice. The times are simulated.
32 devices in a mesh: groups: 2 (over x), dp: 16 (over z, y, core).
Axes of the slice: x: 2, y: 2, z: 4, core: 2. Of those that a mesh axis runs over, the one named last changes fastest.
Arguments:
- tiles: bfloat16 [160, 257, 1280], P(('groups', 'dp')), parts along dimension 0, may hold values from -6 to 6
- counts: int32 [32], P(('groups', 'dp')), parts along dimension 0, may hold values from 1 to 5, as said below
- w_query: bfloat16 [1280, 1280], P(None, 'dp'), may hold values from -10 to 10
- w_keyval: bfloat16 [1280, 2560], replicated, may hold values from -10 to 10
- w_out: bfloat16 [1280, 1280], P('dp'), may hold values from -0.15625 to 0.15625
- w_up: bfloat16 [1280, 5120], P(None, 'dp'), may hold values from -0.15625 to 0.15625
- w_down: bfloat16 [5120, 1280], P('dp'), may hold values from -0.078125 to 0.078125
- gain_attn: float32 [1280], replicated, may hold values from 0.1 to 1.9
- gain_mlp: float32 [1280], replicated, may hold values from 0.1 to 1.9
- gain_post: float32 [1280], replicated, may hold values from 0.1 to 1.9
- bias_post: float32 [1280], replicated, may hold values from -3 to 3
Outputs:
- pooled: float32 [32, 1280], P(('groups', 'dp')), parts along dimension 0
There are 2 independent parts, one for each index of `groups`. A program takes and returns all parts, laid end to end along the dimension named above; an argument that names none is the same for every part. Nothing has to cross between parts.
Inputs may be any that keep to these rules, and one draw needn't show every extreme that they name: `counts`: some rollout has exactly 5 tiles and some exactly 1.
All inputs are finite; a program needn't handle non-finite values.
Results may differ from a plain program's by a relative error of at most 0.0046.
Values may be sent and summed in bfloat16 or wider, within the bound.
A program may use at most 64 MiB of HBM per device.

v0:
```python
import math

import jax
import jax.numpy as jnp
from jax import lax
from jax.sharding import PartitionSpec as P

HEADS = 16
HEAD_DIM = 80


epsilon = 1e-05


def layer_norm(values, gain):
    centre = jnp.mean(values, axis=-1, keepdims=True)
    centred = values - centre
    spread_sq = jnp.mean(centred * centred, axis=-1, keepdims=True)
    return centred * lax.rsqrt(spread_sq + epsilon) * gain


def head_mix(query_row, keyval):
    features = query_row.shape[0]
    keys = keyval[:, :features].astype(jnp.float32).reshape(-1, HEADS, HEAD_DIM)
    values = keyval[:, features:].astype(jnp.float32).reshape(-1, HEADS, HEAD_DIM)
    heads = query_row.astype(jnp.float32).reshape(HEADS, HEAD_DIM)
    scores = jnp.einsum("hd,thd->ht", heads, keys) / math.sqrt(HEAD_DIM)
    weights = jax.nn.softmax(scores, axis=-1).astype(jnp.bfloat16)
    mixing = jnp.einsum("ht,thd->hd", weights.astype(jnp.float32), values)
    return mixing.reshape(-1).astype(jnp.bfloat16)


def shards(
    tiles, counts, w_query, w_keyval, w_out, w_up, w_down, gain_attn, gain_mlp, gain_post, bias_post
):
    slot_count = tiles.shape[0]
    features = tiles.shape[2]
    rollouts_here = counts.shape[0]
    tile_limit = slot_count // rollouts_here
    axis_count = lax.axis_size("dp")
    device_index = lax.axis_index("dp")
    class_rows = layer_norm(tiles[:, 0, :].astype(jnp.float32), gain_attn).astype(jnp.bfloat16)
    queries = jnp.dot(
        class_rows,
        lax.all_gather(w_query, "dp", axis=1, tiled=True),
        preferred_element_type=jnp.float32,
    ).astype(jnp.bfloat16)
    slot_ids = jnp.arange(slot_count, dtype=jnp.int32)
    slot_live = slot_ids % tile_limit < jnp.repeat(counts, tile_limit)
    ordering = jnp.argsort(jnp.where(slot_live, 0, 1) * slot_count + slot_ids)
    tile_buffer = tiles[ordering]
    query_buffer = queries[ordering]
    anchors = device_index * slot_count + ordering
    held_count = jnp.sum(counts)

    def attend(slot_index, mixing):
        single = lax.dynamic_index_in_dim(tile_buffer, slot_index, 0, keepdims=False)
        normed = layer_norm(single.astype(jnp.float32), gain_attn).astype(jnp.bfloat16)
        keyval = jnp.dot(normed, w_keyval, preferred_element_type=jnp.float32).astype(jnp.bfloat16)
        query_row = lax.dynamic_index_in_dim(query_buffer, slot_index, 0, keepdims=False)
        return lax.dynamic_update_index_in_dim(mixing, head_mix(query_row, keyval), slot_index, 0)

    mixed = lax.fori_loop(0, held_count, attend, jnp.zeros((slot_count, features), jnp.bfloat16))
    total_slots = axis_count * slot_count
    anchor_tags = jnp.where(slot_ids < held_count, anchors, total_slots)
    all_mixed, all_first, all_tags = (
        lax.all_gather(mixed, "dp", axis=0, tiled=True),
        lax.all_gather(tile_buffer[:, 0, :], "dp", axis=0, tiled=True),
        lax.all_gather(anchor_tags, "dp", axis=0, tiled=True),
    )
    mixed_owned = (
        jnp.zeros((total_slots, features), jnp.bfloat16).at[all_tags].set(all_mixed, mode="drop")
    )
    first_owned = (
        jnp.zeros((total_slots, features), jnp.bfloat16).at[all_tags].set(all_first, mode="drop")
    )
    rows_here = w_out.shape[0]
    column_block = lax.dynamic_slice_in_dim(mixed_owned, device_index * rows_here, rows_here, 1)
    partial_out = jnp.dot(column_block, w_out, preferred_element_type=jnp.float32)
    settled = first_owned.astype(jnp.float32) + lax.psum(partial_out, "dp")
    inner = layer_norm(settled, gain_mlp).astype(jnp.bfloat16)
    hidden = jax.nn.gelu(
        jnp.dot(inner, w_up, preferred_element_type=jnp.float32), approximate=False
    ).astype(jnp.bfloat16)
    feed_sum = lax.psum_scatter(
        jnp.dot(hidden, w_down, preferred_element_type=jnp.float32),
        "dp",
        scatter_dimension=0,
        tiled=True,
    )
    outcome = lax.dynamic_slice_in_dim(settled, device_index * slot_count, slot_count, 0) + feed_sum
    final = layer_norm(outcome, gain_post) + bias_post
    final = final.reshape(rollouts_here, tile_limit, features)
    present = (jnp.arange(tile_limit, dtype=jnp.int32)[None, :] < counts[:, None]).astype(
        jnp.float32
    )
    summed = jnp.sum(final * present[:, :, None], axis=1)
    return summed / counts.astype(jnp.float32)[:, None]


def solution(mesh):
    placed = (
        P(("groups", "dp"), None, None),
        P(("groups", "dp")),
        P(None, "dp"),
        P(),
        P("dp", None),
        P(None, "dp"),
        P("dp", None),
        P(),
        P(),
        P(),
        P(),
    )
    return jax.shard_map(
        shards, mesh=mesh, in_specs=placed, out_specs=P(("groups", "dp"), None), check_vma=False
    )
```

profile of v0, /device:TPU:0, one launch (start us, length us, event | category | flops | bytes accessed | tf_op | source)
XLA Modules:
  0.0 329.8 jit_solution(14257588729276614775)
XLA Ops:
  6.5 0.7 all-gather.4.cloned.1.call-update
  8.0 0.9 slice.13
  8.9 1.0 sort.17
  9.9 1.4 fusion.116
  12.2 4.6 %gather_fusion = bf16[5,257,1280]{2,1,0:T(8,128)(2,1)} fusion(bf16[5,257,1280]{2,1,0:T(8,128)(2,1)} %param.13, s32[1024]{0:T(1024)S(1)} %pad_clamp_fusion), kind=kCustom, calls=%fused_computation | custom fusion | bytes 6579220 | tf_op jit(solution)/shard_map/gather | solution.py:51
  16.8 13.9 %all-reduce = s32[80]{0:T(128)S(1)} all-reduce(s32[80]{0:T(128)S(1)} %get-tuple-element.76), channel_id=1, replica_groups=mesh['groups'=2,'dp'=16] {'dp'}, use_global_device_ids=true, to_apply=%add | all-reduce | flops 80 | bytes 640
  30.8 0.2 fusion.71
  31.0 27.3 %all-gather.4.cloned.1.call-done = bf16[1280,1280]{0,1:T(8,128)(2,1)} async-done(((bf16[1280,80]{0,1:T(8,128)(2,1)}), bf16[1280,1280]{0,1:T(8,128)(2,1)}) %all-gather.4.cloned.1.call-update) | async-done | bytes 3276816 | tf_op jit(solution)/shard_map/all_gather | solution.py:45
  58.3 2.9 convolution_convert_fusion.1
  61.2 0.6 gather_fusion.1
  61.8 12.1 %while.10 = (s32[]{:T(128)}, bf16[5,1280]{1,0:T(8,128)(2,1)S(1)}, s32[]{:T(128)}, bf16[5,1280]{1,0:T(8,128)(2,1)S(1)}, bf16[5,257,1280]{2,1,0:T(8,128)(2,1)}, /*...) while((s32[]{:T(128)}, bf16[5,1280]{1,0:T(8,128)(2,1)S(1)}, ...), condition=%wide.region_9.10_spmd, body=%wide.region_4.9_spmd.sunk | while | flops 1689905920 | bytes 16573255 | solution.py:63
  62.5 1.3 convert_reduce_fusion.3
  63.8 1.4 fusion.145
  65.2 5.2 %convolution_convert_fusion.3 = bf16[257,2560]{1,0:T(8,128)(2,1)S(1)} fusion(bf16[1280,2560]{1,0:T(8,128)(2,1)} %get-tuple-element.151, f32[1280]{0:T(1024)S(1)} %get-tuple-element.150, f32[257]{0:T(512)S(1)} %add_rsqrt_fusion.5, f32[257]{0:T(512)S(1)} %broadcast_multiply_fusion.5, bf16[5,257,1280]{2,1,0:T(8,128)(2,1)} %get-tuple-element.149, ...), kind=kOutput, calls=%fused_computation.4.clone.1 | convolution fusion | flops 1686577920 | bytes 8552460 | tf_op jit(solution)/shard_map/while/body/dot_general | solution.py:59
  70.5 0.6 copy.59
  71.3 0.6 copy.60
  71.9 0.3 fusion.147
  72.3 0.2 fusion.149
  72.6 0.4 fusion.151
  73.9 62.9 %all-gather.1 = bf16[16,5,1280]{2,1,0:T(8,128)(2,1)S(1)} all-gather(bf16[1,5,1280]{2,1,0:T(8,128)(2,1)S(1)} %bitcast.94), channel_id=1, replica_groups=mesh['groups'=2,'dp'=16] {'dp'}, dimensions={0}, use_global_device_ids=true | all-gather | bytes 217600 | tf_op jit(solution)/shard_map/all_gather | solution.py:67
  136.9 1.0 scatter_custom_fusion.1
  137.9 2.0 fusion.75
  140.0 0.9 slice.20
  140.9 18.8 %all-gather = bf16[80,1,1280]{2,1,0:T(2,128)(2,1)S(1)} all-gather(bf16[5,1,1280]{2,1,0:T(2,128)(2,1)S(1)} %slice.20), channel_id=2, replica_groups=mesh['groups'=2,'dp'=16] {'dp'}, dimensions={0}, use_global_device_ids=true | all-gather | bytes 217600 | tf_op jit(solution)/shard_map/all_gather | solution.py:68
  159.6 1.0 scatter_custom_fusion
  160.6 67.1 %all-reduce.5.cloned.1.call-done = f32[80,1280]{1,0:T(8,128)} async-done(((f32[80,1280]{1,0:T(8,128)}), f32[80,1280]{1,0:T(8,128)}) %all-reduce.5.cloned.1.call-update) | async-done | bytes 409616 | tf_op jit(solution)/shard_map/psum | solution.py:80
  227.8 1.1 fusion.114
  228.9 0.2 multiply_reduce_fusion
  229.2 1.9 fusion.34
  231.7 89.6 %all-reduce.7.cloned.1.call-done = f32[80,1280]{1,0:T(8,128)} async-done(((f32[80,1280]{1,0:T(8,128)}), f32[80,1280]{1,0:T(8,128)}) %all-reduce.7.cloned.1.call-update) | async-done | bytes 409616
  321.4 1.0 fusion.113
  322.7 0.6 div.65
  (46 shorter events, 1.5 us)
Async XLA Ops:
  6.5 222.6 %copy-start = (bf16[320,1280]{1,0:T(8,128)(2,1)S(1)}, bf16[320,1280]{1,0:T(8,128)(2,1)}, u32[]{:S(2)}) copy-start(bf16[320,1280]{1,0:T(8,128)(2,1)} %param.19) | copy-start | bytes 2457604
  6.5 51.8 %all-gather.4.cloned.1.call-start = ((), (), s32[]{:S(2)}) async-start(), calls=%async_computation | async-start | bytes 3481600 | tf_op jit(solution)/shard_map/all_gather | solution.py:45
  7.3 220.5 %all-reduce.5.cloned.1.call-start = ((), (), s32[]{:S(2)}) async-start(), calls=%async_computation.1 | async-start | bytes 819200 | tf_op jit(solution)/shard_map/psum | solution.py:80
  12.2 46.1 %copy-start.1 = (f32[1280]{0:T(1024)S(1)}, f32[1280]{0:T(1024)}, u32[]{:S(2)}) copy-start(f32[1280]{0:T(1024)} %param.20) | copy-start | bytes 15364
  73.9 155.3 %copy-start.4 = (bf16[1280,320]{0,1:T(8,128)(2,1)S(1)}, bf16[1280,320]{0,1:T(8,128)(2,1)}, u32[]{:S(2)}) copy-start(bf16[1280,320]{0,1:T(8,128)(2,1)} %param.18) | copy-start | bytes 2457604
  73.9 155.3 %copy-start.5 = (f32[1280]{0:T(1024)S(1)}, f32[1280]{0:T(1024)}, u32[]{:S(2)}) copy-start(f32[1280]{0:T(1024)} %param.21) | copy-start | bytes 15364
  139.9 181.4 %all-reduce.7.cloned.1.call-start = ((), (), s32[]{:S(2)}) async-start(), calls=%async_computation.2 | async-start | bytes 819200
  160.6 162.0 %copy-start.2 = (f32[1280]{0:T(1024)S(1)}, f32[1280]{0:T(1024)}, u32[]{:S(2)}) copy-start(f32[1280]{0:T(1024)} %param.23) | copy-start | bytes 15364
  160.6 162.0 %copy-start.3 = (f32[1280]{0:T(1024)S(1)}, f32[1280]{0:T(1024)}, u32[]{:S(2)}) copy-start(f32[1280]{0:T(1024)} %param.22) | copy-start | bytes 15364
Sparse Core Ops, SparseCore 0:
  9.6 48.6 all-gather.3
  140.0 87.6 all-reduce.4
  231.2 90.1 all-reduce.6
where the time goes:
time: 331 us; the launch traced here: 330 us
  waiting for transfers between devices  185 us (56%)
  blocking collectives  95.6 us (29%)
  between operations  15.3 us (5%)
  local copies, waits for them, and re-layouts  12.8 us (4%)
  matrix products  12.6 us (4%)
  other arithmetic  7.32 us (2%)
    unnamed x4, waiting for transfers between devices  90.4 us
    psum x1, waiting for transfers between devices, shards(): settled = first_owned.astype(jnp.float32) + lax.psum(partial_out, 'dp')  67.1 us
    all_gather x1, blocking collectives, shards(): lax.all_gather(mixed, 'dp', axis=0, tiled=True)  62.9 us
    all_gather x1, waiting for transfers between devices, shards(): lax.all_gather(w_query, 'dp', axis=1, tiled=True)  27.3 us
    all_gather x1, blocking collectives, shards(): lax.all_gather(tile_buffer[:, 0, :], 'dp', axis=0, tiled=True)  18.8 us
    unnamed x1, blocking collectives  13.9 us
  transfers between devices with their start and end apart: 3, of which 3 were waited for; matrix products, arithmetic and copies ran while one was open for 3% of the time, Pallas kernels for 0%

commit v1 on v0

v1 whole, which is shorter than its diff:
```python
import functools
import math

import jax
import jax.numpy as jnp
from jax import lax
from jax.experimental import pallas as pl
from jax.experimental.pallas import tpu as pltpu
from jax.sharding import PartitionSpec as P

HEADS = 16
HEAD_DIM = 80
SLOTS = 5
ROWS = 16
WIDE = 512
GROUP = 256

epsilon = 1e-05
F32 = jnp.float32
BF16 = jnp.bfloat16
MESH = pl.DeviceIdType.MESH


def layer_norm(values, gain):
    centre = jnp.mean(values, axis=-1, keepdims=True)
    centred = values - centre
    spread_sq = jnp.mean(centred * centred, axis=-1, keepdims=True)
    return centred * lax.rsqrt(spread_sq + epsilon) * gain


def erf(x):
    x = jnp.clip(x, -3.832506856900711, 3.832506856900711)
    sq = x * x
    top = jnp.full_like(x, 0.00022905065861350646)
    for c in (
        0.0034082910107109506,
        0.050955695062380861,
        0.18520832239976145,
        1.128379143519084,
    ):
        top = top * sq + c
    low = jnp.full_like(x, -1.1791602954361697e-7)
    for c in (
        0.000023547966471313185,
        0.0010179625278914885,
        0.014070470171167667,
        0.11098505178285362,
        0.49746925110067538,
        1.0,
    ):
        low = low * sq + c
    return x * top / low


def gelu(x):
    return 0.5 * x * (1.0 + erf(x * math.sqrt(0.5)))


def dot(a, b):
    return jnp.dot(a, b, preferred_element_type=F32)


def dot_t(a, b):
    return lax.dot_general(a, b, (((1,), (1,)), ((), ())), preferred_element_type=F32)


def pack_rows(x):
    d = x.shape[1]
    last = jnp.concatenate([x[:, 2 * WIDE :], jnp.zeros((SLOTS, 3 * WIDE - d), F32)], axis=1)
    return jnp.concatenate(
        [x[:, :WIDE], x[:, WIDE : 2 * WIDE], last, jnp.zeros((1, WIDE), F32)], axis=0
    )


def unpack_rows(p, d):
    return jnp.concatenate(
        [p[0:SLOTS], p[SLOTS : 2 * SLOTS], p[2 * SLOTS : 3 * SLOTS, : d - 2 * WIDE]], axis=1
    )


def spread(packed, d):
    size = packed.shape[0]
    r = lax.broadcasted_iota(jnp.int32, (size, size), 0)
    c = lax.broadcasted_iota(jnp.int32, (size, size), 1)
    same = (r >> 4) == (c >> 4)
    rm = r & 15
    slot = rm - jnp.where(rm >= 5, 5, 0) - jnp.where(rm >= 10, 5, 0) - jnp.where(rm >= 15, 5, 0)
    cm = c & 15
    out = []
    for k in range(3):
        pick = jnp.where(same & (cm == slot + 5 * k), 1.0, 0.0).astype(BF16)
        src = packed if k < 2 else packed[:, : d - 2 * WIDE]
        out.append(dot(pick, src).astype(BF16))
    return jnp.concatenate(out, axis=1)


def fold(y):
    size, d = y.shape
    rm = lax.broadcasted_iota(jnp.int32, (size, WIDE), 0) & 15
    last = jnp.concatenate([y[:, 2 * WIDE :], jnp.zeros((size, 3 * WIDE - d), F32)], axis=1)
    return jnp.where(rm < 5, y[:, :WIDE], jnp.where(rm < 10, y[:, WIDE : 2 * WIDE], last))


def kernel(
    n,
    tiles, counts, w_query, w_keyval, w_out, w_up, w_down, gain_attn, gain_mlp, gain_post, bias_post,
    out,
    first_v, tiles_v, normed_v, wq_v, wk_v, wv_v, wo_v, wu_v, wd_v,
    rows_r, q_s, q_r, mix_s, mix_r, out_s, out_r, inner_r, feed_s, feed_r,
    load_sem, send_sem, recv_sem,
):
    me = lax.axis_index("dp")
    tok, d = tiles.shape[1], tiles.shape[2]
    cw = w_query.shape[1]
    total = n * ROWS
    groups = max(total // GROUP, 1)
    size = total // groups

    loads = []

    def load(src, dst):
        copy = pltpu.make_async_copy(src, dst, load_sem.at[len(loads)])
        copy.start()
        loads.append(copy)
        return copy

    load_first = load(tiles.at[:, pl.ds(0, 16), :], first_v)
    load_q = load(w_query, wq_v)
    load_tiles = [load(tiles.at[s], tiles_v.at[s]) for s in range(SLOTS)]
    load_k = load(w_keyval.at[:, pl.ds(0, d)], wk_v)
    load_v = load(w_keyval.at[:, pl.ds(d, d)], wv_v)
    load_o = load(w_out, wo_v)
    load_u = load(w_up, wu_v)
    load_d = load(w_down, wd_v)

    barrier = pltpu.get_barrier_semaphore()

    def greet(k, _):
        peer = lax.rem(me + k, n)
        pl.semaphore_signal(barrier, inc=1, device_id={"dp": peer}, device_id_type=MESH)
        return 0

    lax.fori_loop(1, n, greet, 0)

    def send_all(src_at, dst, phase):
        def body(k, _):
            peer = lax.rem(me + k, n)
            pltpu.make_async_remote_copy(
                src_ref=src_at(peer),
                dst_ref=dst.at[me],
                send_sem=send_sem.at[phase],
                recv_sem=recv_sem.at[phase],
                device_id={"dp": peer},
                device_id_type=MESH,
            ).start()
            return 0

        lax.fori_loop(1, n, body, 0)

    def wait_all(ref, sem):
        part = ref.at[pl.ds(0, n - 1)]
        pltpu.make_async_copy(part, part, sem).wait()

    g_attn = gain_attn[...].reshape(1, d)

    load_first.wait()
    first = jnp.concatenate([first_v[s, 0:1, :].astype(F32) for s in range(SLOTS)], axis=0)
    rows_r[me] = pack_rows(layer_norm(first, g_attn)).astype(BF16)
    pl.semaphore_wait(barrier, n - 1)
    send_all(lambda peer: rows_r.at[me], rows_r, 0)

    def norm_tile(s):
        load_tiles[s].wait()

        def body(i, _):
            at = pl.ds(pl.multiple_of(i * 32, 32), 32)
            normed_v[s, at, :] = layer_norm(tiles_v[s, at, :].astype(F32), g_attn).astype(BF16)
            return 0

        lax.fori_loop(0, tok // 32, body, 0, unroll=2)
        whole = tok // 32 * 32
        rest = tok - whole
        tail = layer_norm(tiles_v[s, whole:tok, :].astype(F32), g_attn)
        tail = jnp.concatenate(
            [tail, jnp.zeros((normed_v.shape[1] - tok, d), F32)], axis=0
        )
        normed_v[s, whole:, :] = tail.astype(BF16)

    for s in range(3):
        norm_tile(s)

    load_q.wait()
    wait_all(rows_r, recv_sem.at[0])
    for g in range(groups):
        owners = size // ROWS
        packed = rows_r[g * owners : (g + 1) * owners].reshape(size, WIDE)
        q = dot(spread(packed, d), wq_v[...]).astype(BF16)
        q_s[g * owners : (g + 1) * owners] = q.reshape(owners, ROWS, cw)
    send_all(lambda peer: q_s.at[peer], q_r, 1)
    q_r[me] = q_s[me]

    for s in range(3, SLOTS):
        norm_tile(s)

    load_k.wait()
    wait_all(q_r, recv_sem.at[1])
    query = jnp.concatenate([q_r[i].astype(F32) for i in range(n)], axis=1)
    head_row = lax.broadcasted_iota(jnp.int32, (HEADS, d), 0)
    lane = lax.broadcasted_iota(jnp.int32, (HEADS, d), 1)
    own_head = (lane >= head_row * HEAD_DIM) & (lane < (head_row + 1) * HEAD_DIM)
    apart = jnp.concatenate(
        [jnp.where(own_head, query[s : s + 1], 0.0).astype(BF16) for s in range(SLOTS)], axis=0
    )
    keyed = dot_t(apart, wk_v[...]).astype(BF16)
    padded = normed_v.shape[1]
    real = lax.broadcasted_iota(jnp.int32, (HEADS, padded), 1) < tok
    context = []
    for s in range(SLOTS):
        scores = dot_t(keyed[s * HEADS : (s + 1) * HEADS], normed_v[s]) / math.sqrt(HEAD_DIM)
        scores = jnp.where(real, scores, -jnp.inf)
        weights = jnp.exp(scores - jnp.max(scores, axis=-1, keepdims=True))
        weights = weights / jnp.sum(weights, axis=-1, keepdims=True)
        context.append(dot(weights.astype(BF16), normed_v[s]).astype(BF16))
    load_v.wait()
    valued = dot(jnp.concatenate(context, axis=0), wv_v[...])
    mixed = jnp.concatenate(
        [
            jnp.sum(
                jnp.where(own_head, valued[s * HEADS : (s + 1) * HEADS], 0.0),
                axis=0,
                keepdims=True,
            )
            for s in range(SLOTS)
        ],
        axis=0,
    )
    thrice = jnp.concatenate([mixed, mixed, mixed, mixed[0:1]], axis=0)
    for i in range(n):
        mix_s[i] = thrice[:, i * cw : (i + 1) * cw].astype(BF16)
    send_all(lambda peer: mix_s.at[peer], mix_r, 2)
    mix_r[me] = mix_s[me]

    load_o.wait()
    wait_all(mix_r, recv_sem.at[2])
    owners = size // ROWS
    for g in range(groups):
        at = slice(g * owners, (g + 1) * owners)
        part = dot(mix_r[at].reshape(size, cw), wo_v[...])
        out_s[at] = fold(part).astype(BF16).reshape(owners, ROWS, WIDE)
    send_all(lambda peer: out_s.at[peer], out_r, 3)
    out_r[me] = out_s[me]
    wait_all(out_r, recv_sem.at[3])

    def total_of(ref):
        acc = ref[0].astype(F32)
        for i in range(1, n):
            acc = acc + ref[i].astype(F32)
        return unpack_rows(acc, d)

    settled = first + total_of(out_r)
    inner = layer_norm(settled, gain_mlp[...].reshape(1, d))
    inner_r[me] = pack_rows(inner).astype(BF16)
    send_all(lambda peer: inner_r.at[me], inner_r, 4)
    load_u.wait()
    load_d.wait()
    wait_all(inner_r, recv_sem.at[4])
    for g in range(groups):
        at = slice(g * owners, (g + 1) * owners)
        rows = spread(inner_r[at].reshape(size, WIDE), d)
        hidden = gelu(dot(rows, wu_v[...])).astype(BF16)
        feed_s[at] = fold(dot(hidden, wd_v[...])).astype(BF16).reshape(owners, ROWS, WIDE)
    send_all(lambda peer: feed_s.at[peer], feed_r, 5)
    feed_r[me] = feed_s[me]
    wait_all(feed_r, recv_sem.at[5])

    outcome = settled + total_of(feed_r)
    final = layer_norm(outcome, gain_post[...].reshape(1, d)) + bias_post[...].reshape(1, d)
    count = counts[0]
    present = lax.broadcasted_iota(jnp.int32, (SLOTS, d), 0) < count
    summed = jnp.sum(jnp.where(present, final, 0.0), axis=0, keepdims=True)
    out[...] = summed / jnp.full((1, d), count, jnp.int32).astype(F32)

    for phase, ref in enumerate((rows_r, q_s, mix_s, out_s, inner_r, feed_s)):
        wait_all(ref, send_sem.at[phase])


def shards(
    tiles, counts, w_query, w_keyval, w_out, w_up, w_down, gain_attn, gain_mlp, gain_post, bias_post
):
    n = lax.axis_size("dp")
    slots, tok, d = tiles.shape
    cw = w_query.shape[1]
    padded = (tok + 15) // 16 * 16
    anywhere = pl.BlockSpec(memory_space=pl.ANY)
    vmem = pl.BlockSpec(memory_space=pltpu.VMEM)
    smem = pl.BlockSpec(memory_space=pltpu.SMEM)
    message = pltpu.VMEM((n, ROWS, WIDE), BF16)
    narrow = pltpu.VMEM((n, ROWS, cw), BF16)
    return pl.pallas_call(
        functools.partial(kernel, n),
        out_shape=jax.ShapeDtypeStruct((counts.shape[0], d), F32),
        in_specs=[anywhere, smem] + [anywhere] * 5 + [vmem] * 4,
        out_specs=vmem,
        scratch_shapes=[
            pltpu.VMEM((slots, 16, d), BF16),
            pltpu.VMEM((slots, tok, d), BF16),
            pltpu.VMEM((slots, padded, d), BF16),
            pltpu.VMEM(w_query.shape, BF16),
            pltpu.VMEM((d, d), BF16),
            pltpu.VMEM((d, d), BF16),
            pltpu.VMEM(w_out.shape, BF16),
            pltpu.VMEM(w_up.shape, BF16),
            pltpu.VMEM(w_down.shape, BF16),
            message, narrow, narrow, narrow, narrow, message, message, message, message, message,
            pltpu.SemaphoreType.DMA((12,)),
            pltpu.SemaphoreType.DMA((6,)),
            pltpu.SemaphoreType.DMA((6,)),
        ],
        compiler_params=pltpu.CompilerParams(
            collective_id=0, has_side_effects=True, vmem_limit_bytes=50 * 1024 * 1024
        ),
    )(tiles, counts, w_query, w_keyval, w_out, w_up, w_down, gain_attn, gain_mlp, gain_post, bias_post)


def solution(mesh):
    placed = (
        P(("groups", "dp"), None, None),
        P(("groups", "dp")),
        P(None, "dp"),
        P(),
        P("dp", None),
        P(None, "dp"),
        P("dp", None),
        P(),
        P(),
        P(),
        P(),
    )
    return jax.shard_map(
        shards, mesh=mesh, in_specs=placed, out_specs=P(("groups", "dp"), None), check_vma=False
    )
```

time: 331 us -> 60.4 us (0.18)
  waiting for transfers between devices: 185 us -> 0 us
  blocking collectives: 95.6 us -> 0 us
  Pallas kernels: 0 us -> 51.1 us
  between operations: 15.3 us -> 0.69 us
  matrix products: 12.6 us -> 0 us
  other arithmetic: 7.32 us -> 0 us
  local copies, waits for them, and re-layouts: 12.8 us -> 8.15 us
    unnamed x4 -> x0, waiting for transfers between devices: 90.4 us -> none
    all_gather x2 -> x0, blocking collectives: 81.7 us -> none  [the longest x1 62.9 us: shards(): lax.all_gather(mixed, 'dp', axis=0, tiled=True)]
    psum x1 -> x0, waiting for transfers between devices: 67.1 us -> none  [shards(): settled = first_owned.astype(jnp.float32) + lax.psum(partial_out, 'dp')]
    pallas_call x0 -> x1, Pallas kernels: none -> 51.1 us  [shards(): pl.pallas_call(functools.partial(kernel, n), out_shape=jax.ShapeDtypeStru...]
    all_gather x1 -> x0, waiting for transfers between devices: 27.3 us -> none  [shards(): lax.all_gather(w_query, 'dp', axis=1, tiled=True)]
    unnamed x1 -> x0, blocking collectives: 13.9 us -> none
    dot_general x6 -> x0, matrix products: 12.6 us -> none  [the longest x1 5.17 us: attend(): jnp.dot(normed, w_keyval, preferred_element_type=jnp.float32)]
    unnamed x15, local copies, waits for them, and re-layouts: 1.52 us -> 8.15 us
  transfers between devices with their start and end apart: 3 -> 0, of which waited for: 3 -> 0; matrix products, arithmetic and copies ran while one was open for 3% -> 0% of each run, Pallas kernels for 0% -> 0%
where the time goes in v1:
time: 60.4 us; the launch traced here: 59.9 us
  Pallas kernels  51.1 us (85%)
  local copies, waits for them, and re-layouts  8.15 us (13%)
  between operations  0.69 us (1%)
    pallas_call x1, Pallas kernels, shards(): pl.pallas_call(functools.partial(kernel, n), out_shape=jax.ShapeDtypeStru...  51.1 us
    unnamed x15, local copies, waits for them, and re-layouts  8.15 us

profile of v1, /device:TPU:0, one launch (start us, length us, event | category | flops | bytes accessed | tf_op | source)
XLA Modules:
  0.0 59.9 jit_solution(2988505577139606155)
XLA Ops:
  0.7 1.1 %copy.12.w_query = bf16[1280,80]{1,0:T(8,128)(2,1)S(1)} copy(bf16[1280,80]{0,1:T(8,128)(2,1)} %param.13) | data formatting | bytes 409600 | tf_op args[2]
  1.8 1.6 %copy.13.w_up = bf16[1280,320]{1,0:T(8,128)(2,1)S(1)} copy(bf16[1280,320]{0,1:T(8,128)(2,1)} %param.16) | data formatting | bytes 1638400 | tf_op args[5]
  3.4 0.0 copy-start
  3.4 1.1 %copy-done = bf16[320,1280]{1,0:T(8,128)(2,1)S(1)} copy-done((bf16[320,1280]{1,0:T(8,128)(2,1)S(1)}, bf16[320,1280]{1,0:T(8,128)(2,1)}, u32[]{:S(2)}) %copy-start) | copy-done | bytes 819224
  4.5 0.0 copy-start.1
  4.5 0.9 %copy-done.1 = bf16[80,1280]{1,0:T(8,128)(2,1)S(1)} copy-done((bf16[80,1280]{1,0:T(8,128)(2,1)S(1)}, bf16[80,1280]{1,0:T(8,128)(2,1)}, u32[]{:S(2)}) %copy-start.1) | copy-done | bytes 204824
  5.4 0.0 copy-start.2
  5.4 0.7 %copy-done.2 = f32[1280]{0:T(1024)S(1)} copy-done((f32[1280]{0:T(1024)S(1)}, f32[1280]{0:T(1024)}, u32[]{:S(2)}) %copy-start.2) | copy-done | bytes 5144
  6.1 0.0 copy-start.3
  6.1 0.7 %copy-done.3 = f32[1280]{0:T(1024)S(1)} copy-done((f32[1280]{0:T(1024)S(1)}, f32[1280]{0:T(1024)}, u32[]{:S(2)}) %copy-start.3) | copy-done | bytes 5144
  6.8 0.0 copy-start.4
  6.8 0.7 %copy-done.4 = f32[1280]{0:T(1024)S(1)} copy-done((f32[1280]{0:T(1024)S(1)}, f32[1280]{0:T(1024)}, u32[]{:S(2)}) %copy-start.4) | copy-done | bytes 5144
  7.5 0.0 copy-start.5
  7.5 0.7 %copy-done.5 = f32[1280]{0:T(1024)S(1)} copy-done((f32[1280]{0:T(1024)S(1)}, f32[1280]{0:T(1024)}, u32[]{:S(2)}) %copy-start.5) | copy-done | bytes 5144
  8.2 51.1 %shard_map.109 = f32[1,1280]{1,0:T(1,128)S(1)} custom-call(bf16[5,257,1280]{2,1,0:T(8,128)(2,1)} %tiles.1, s32[1]{0:T(128)S(6)} %copy.15.counts, bf16[1280,80]{1,0:T(8,128)(2,1)S(1)} %copy.12.w_query, bf16[1280,2560]{1,0:T(8,128)(2,1)} %w_keyval.1, bf16[80,1280]{1,0:T(8,128)(2,1)S(1)} %copy-done.1, bf16[1280,320]{1,0:T(8,128)(2,1)S(1)} %copy.13.w_up, ...), custom_call_target="tpu_custom_call" | custom-call | tf_op jit(solution)/shard_map/pallas_call | solution.py:299
  59.3 0.6 copy.16
Async XLA Ops:
  3.4 1.1 %copy-start = (bf16[320,1280]{1,0:T(8,128)(2,1)S(1)}, bf16[320,1280]{1,0:T(8,128)(2,1)}, u32[]{:S(2)}) copy-start(bf16[320,1280]{1,0:T(8,128)(2,1)} %w_down.1) | copy-start | bytes 2457604
  4.5 0.9 %copy-start.1 = (bf16[80,1280]{1,0:T(8,128)(2,1)S(1)}, bf16[80,1280]{1,0:T(8,128)(2,1)}, u32[]{:S(2)}) copy-start(bf16[80,1280]{1,0:T(8,128)(2,1)} %w_out.1) | copy-start | bytes 614404
  5.4 0.7 %copy-start.2 = (f32[1280]{0:T(1024)S(1)}, f32[1280]{0:T(1024)}, u32[]{:S(2)}) copy-start(f32[1280]{0:T(1024)} %gain_attn.1) | copy-start | bytes 15364
  6.1 0.7 %copy-start.3 = (f32[1280]{0:T(1024)S(1)}, f32[1280]{0:T(1024)}, u32[]{:S(2)}) copy-start(f32[1280]{0:T(1024)} %gain_mlp.1) | copy-start | bytes 15364
  6.8 0.7 %copy-start.4 = (f32[1280]{0:T(1024)S(1)}, f32[1280]{0:T(1024)}, u32[]{:S(2)}) copy-start(f32[1280]{0:T(1024)} %gain_post.1) | copy-start | bytes 15364
  7.5 0.7 %copy-start.5 = (f32[1280]{0:T(1024)S(1)}, f32[1280]{0:T(1024)}, u32[]{:S(2)}) copy-start(f32[1280]{0:T(1024)} %bias_post.1) | copy-start | bytes 15364

commit v2 on v1

--- a/solution.py
+++ b/solution.py
@@ -105,13 +105,13 @@
     n,
     tiles, counts, w_query, w_keyval, w_out, w_up, w_down, gain_attn, gain_mlp, gain_post, bias_post,
     out,
-    first_v, tiles_v, normed_v, wq_v, wk_v, wv_v, wo_v, wu_v, wd_v,
+    gains_v, first_v, tiles_v, normed_v, wq_v, wk_v, wv_v, wo_v, wu_v, wd_v,
     rows_r, q_s, q_r, mix_s, mix_r, out_s, out_r, inner_r, feed_s, feed_r,
     load_sem, send_sem, recv_sem,
 ):
     me = lax.axis_index("dp")
     tok, d = tiles.shape[1], tiles.shape[2]
-    cw = w_query.shape[1]
+    cw = w_query.shape[0]
     total = n * ROWS
     groups = max(total // GROUP, 1)
     size = total // groups
@@ -124,6 +124,10 @@
         loads.append(copy)
         return copy
 
+    load_gains = [
+        load(ref, gains_v.at[i])
+        for i, ref in enumerate((gain_attn, gain_mlp, gain_post, bias_post))
+    ]
     load_first = load(tiles.at[:, pl.ds(0, 16), :], first_v)
     load_q = load(w_query, wq_v)
     load_tiles = [load(tiles.at[s], tiles_v.at[s]) for s in range(SLOTS)]
@@ -161,7 +165,9 @@
         part = ref.at[pl.ds(0, n - 1)]
         pltpu.make_async_copy(part, part, sem).wait()
 
-    g_attn = gain_attn[...].reshape(1, d)
+    for copy in load_gains:
+        copy.wait()
+    g_attn, g_mlp, g_post, b_post = [gains_v[i].reshape(1, d) for i in range(4)]
 
     load_first.wait()
     first = jnp.concatenate([first_v[s, 0:1, :].astype(F32) for s in range(SLOTS)], axis=0)
@@ -194,7 +200,7 @@
     for g in range(groups):
         owners = size // ROWS
         packed = rows_r[g * owners : (g + 1) * owners].reshape(size, WIDE)
-        q = dot(spread(packed, d), wq_v[...]).astype(BF16)
+        q = dot_t(spread(packed, d), wq_v[...]).astype(BF16)
         q_s[g * owners : (g + 1) * owners] = q.reshape(owners, ROWS, cw)
     send_all(lambda peer: q_s.at[peer], q_r, 1)
     q_r[me] = q_s[me]
@@ -258,7 +264,7 @@
         return unpack_rows(acc, d)
 
     settled = first + total_of(out_r)
-    inner = layer_norm(settled, gain_mlp[...].reshape(1, d))
+    inner = layer_norm(settled, g_mlp)
     inner_r[me] = pack_rows(inner).astype(BF16)
     send_all(lambda peer: inner_r.at[me], inner_r, 4)
     load_u.wait()
@@ -267,14 +273,14 @@
     for g in range(groups):
         at = slice(g * owners, (g + 1) * owners)
         rows = spread(inner_r[at].reshape(size, WIDE), d)
-        hidden = gelu(dot(rows, wu_v[...])).astype(BF16)
+        hidden = gelu(dot_t(rows, wu_v[...])).astype(BF16)
         feed_s[at] = fold(dot(hidden, wd_v[...])).astype(BF16).reshape(owners, ROWS, WIDE)
     send_all(lambda peer: feed_s.at[peer], feed_r, 5)
     feed_r[me] = feed_s[me]
     wait_all(feed_r, recv_sem.at[5])
 
     outcome = settled + total_of(feed_r)
-    final = layer_norm(outcome, gain_post[...].reshape(1, d)) + bias_post[...].reshape(1, d)
+    final = layer_norm(outcome, g_post) + b_post
     count = counts[0]
     present = lax.broadcasted_iota(jnp.int32, (SLOTS, d), 0) < count
     summed = jnp.sum(jnp.where(present, final, 0.0), axis=0, keepdims=True)
@@ -290,6 +296,7 @@
     n = lax.axis_size("dp")
     slots, tok, d = tiles.shape
     cw = w_query.shape[1]
+    w_query, w_up = w_query.T, w_up.T
     padded = (tok + 15) // 16 * 16
     anywhere = pl.BlockSpec(memory_space=pl.ANY)
     vmem = pl.BlockSpec(memory_space=pltpu.VMEM)
@@ -299,9 +306,10 @@
     return pl.pallas_call(
         functools.partial(kernel, n),
         out_shape=jax.ShapeDtypeStruct((counts.shape[0], d), F32),
-        in_specs=[anywhere, smem] + [anywhere] * 5 + [vmem] * 4,
+        in_specs=[anywhere, smem] + [anywhere] * 9,
         out_specs=vmem,
         scratch_shapes=[
+            pltpu.VMEM((4, d), F32),
             pltpu.VMEM((slots, 16, d), BF16),
             pltpu.VMEM((slots, tok, d), BF16),
             pltpu.VMEM((slots, padded, d), BF16),
@@ -312,12 +320,12 @@
             pltpu.VMEM(w_up.shape, BF16),
             pltpu.VMEM(w_down.shape, BF16),
             message, narrow, narrow, narrow, narrow, message, message, message, message, message,
-            pltpu.SemaphoreType.DMA((12,)),
+            pltpu.SemaphoreType.DMA((16,)),
             pltpu.SemaphoreType.DMA((6,)),
             pltpu.SemaphoreType.DMA((6,)),
         ],
         compiler_params=pltpu.CompilerParams(
-            collective_id=0, has_side_effects=True, vmem_limit_bytes=50 * 1024 * 1024
+            collective_id=0, has_side_effects=True, vmem_limit_bytes=60 * 1024 * 1024
         ),
     )(tiles, counts, w_query, w_keyval, w_out, w_up, w_down, gain_attn, gain_mlp, gain_post, bias_post)
 

time: 60.4 us -> 53.3 us (0.88)
  local copies, waits for them, and re-layouts: 8.15 us -> 1.28 us
    unnamed x15 -> x1, local copies, waits for them, and re-layouts: 8.15 us -> 1.28 us
where the time goes in v2:
time: 53.3 us; the launch traced here: 52.9 us
  Pallas kernels  51 us (96%)
  local copies, waits for them, and re-layouts  1.28 us (2%)
  between operations  0.66 us (1%)
    pallas_call x1, Pallas kernels, shards(): pl.pallas_call(functools.partial(kernel, n), out_shape=jax.ShapeDtypeStru...  51 us
    unnamed x1, local copies, waits for them, and re-layouts  1.28 us

profile of v2, /device:TPU:0, one launch (start us, length us, event | category | flops | bytes accessed | tf_op | source)
XLA Modules:
  0.0 52.9 jit_solution(10575925000604073387)
XLA Ops:
  0.7 51.0 %shard_map.109 = f32[1,1280]{1,0:T(1,128)} custom-call(bf16[5,257,1280]{2,1,0:T(8,128)(2,1)} %tiles.1, s32[1]{0:T(128)S(6)} %copy.13.counts, bf16[80,1280]{1,0:T(8,128)(2,1)} %bitcast.3, bf16[1280,2560]{1,0:T(8,128)(2,1)} %w_keyval.1, bf16[80,1280]{1,0:T(8,128)(2,1)} %w_out.1, bf16[320,1280]{1,0:T(8,128)(2,1)} %bitcast.2, bf16[320,1280]{1,0:T(8,128)(2,1)} %w_down.1, ...), custom_call_target="tpu_custom_call" | custom-call | tf_op jit(solution)/shard_map/pallas_call | solution.py:306
  51.7 1.3 %copy.14 = f32[1,1280]{1,0:T(1,128)} copy(f32[1,1280]{1,0:T(1,128)} %shard_map.109) | data formatting | bytes 10240

commit v3 on v2

--- a/solution.py
+++ b/solution.py
@@ -107,12 +107,16 @@
     out,
     gains_v, first_v, tiles_v, normed_v, wq_v, wk_v, wv_v, wo_v, wu_v, wd_v,
     rows_r, q_s, q_r, mix_s, mix_r, out_s, out_r, inner_r, feed_s, feed_r,
-    load_sem, send_sem, recv_sem,
+    load_sem, send_sem, recv_sem, weight_send, weight_recv,
 ):
     me = lax.axis_index("dp")
     tok, d = tiles.shape[1], tiles.shape[2]
     cw = w_query.shape[0]
-    total = n * ROWS
+    core = lax.rem(me, 2)
+    sibling = me + 1 - 2 * core
+    chips = n // 2
+    chip = lax.div(me, 2)
+    total = chips * ROWS
     groups = max(total // GROUP, 1)
     size = total // groups
 
@@ -129,40 +133,41 @@
         for i, ref in enumerate((gain_attn, gain_mlp, gain_post, bias_post))
     ]
     load_first = load(tiles.at[:, pl.ds(0, 16), :], first_v)
-    load_q = load(w_query, wq_v)
+    load_q = load(w_query, wq_v.at[core])
     load_tiles = [load(tiles.at[s], tiles_v.at[s]) for s in range(SLOTS)]
     load_k = load(w_keyval.at[:, pl.ds(0, d)], wk_v)
     load_v = load(w_keyval.at[:, pl.ds(d, d)], wv_v)
-    load_o = load(w_out, wo_v)
-    load_u = load(w_up, wu_v)
-    load_d = load(w_down, wd_v)
+    load_o = load(w_out, wo_v.at[core])
+    load_u = load(w_up, wu_v.at[core])
+    load_d = load(w_down, wd_v.at[core])
 
     barrier = pltpu.get_barrier_semaphore()
 
     def greet(k, _):
-        peer = lax.rem(me + k, n)
+        peer = lax.rem(chip + k, chips) * 2 + core
         pl.semaphore_signal(barrier, inc=1, device_id={"dp": peer}, device_id_type=MESH)
         return 0
 
-    lax.fori_loop(1, n, greet, 0)
+    pl.semaphore_signal(barrier, inc=1, device_id={"dp": sibling}, device_id_type=MESH)
+    lax.fori_loop(1, chips, greet, 0)
 
     def send_all(src_at, dst, phase):
         def body(k, _):
-            peer = lax.rem(me + k, n)
+            peer = lax.rem(chip + k, chips)
             pltpu.make_async_remote_copy(
                 src_ref=src_at(peer),
-                dst_ref=dst.at[me],
+                dst_ref=dst.at[chip],
                 send_sem=send_sem.at[phase],
                 recv_sem=recv_sem.at[phase],
-                device_id={"dp": peer},
+                device_id={"dp": peer * 2 + core},
                 device_id_type=MESH,
             ).start()
             return 0
 
-        lax.fori_loop(1, n, body, 0)
+        lax.fori_loop(1, chips, body, 0)
 
     def wait_all(ref, sem):
-        part = ref.at[pl.ds(0, n - 1)]
+        part = ref.at[pl.ds(0, chips - 1)]
         pltpu.make_async_copy(part, part, sem).wait()
 
     for copy in load_gains:
@@ -171,9 +176,23 @@
 
     load_first.wait()
     first = jnp.concatenate([first_v[s, 0:1, :].astype(F32) for s in range(SLOTS)], axis=0)
-    rows_r[me] = pack_rows(layer_norm(first, g_attn)).astype(BF16)
-    pl.semaphore_wait(barrier, n - 1)
-    send_all(lambda peer: rows_r.at[me], rows_r, 0)
+    rows_r[chip] = pack_rows(layer_norm(first, g_attn)).astype(BF16)
+    pl.semaphore_wait(barrier, chips)
+    send_all(lambda peer: rows_r.at[chip], rows_r, 0)
+
+    shared = []
+    for k, (src, dst) in enumerate(((w_query, wq_v), (w_out, wo_v), (w_up, wu_v), (w_down, wd_v))):
+        copy = pltpu.make_async_remote_copy(
+            src_ref=src,
+            dst_ref=dst.at[core],
+            send_sem=weight_send.at[k],
+            recv_sem=weight_recv.at[k],
+            device_id={"dp": sibling},
+            device_id_type=MESH,
+        )
+        copy.start()
+        shared.append(copy)
+    share_q, share_o, share_u, share_d = shared
 
     def norm_tile(s):
         load_tiles[s].wait()
@@ -196,21 +215,24 @@
         norm_tile(s)
 
     load_q.wait()
+    share_q.wait_recv()
     wait_all(rows_r, recv_sem.at[0])
     for g in range(groups):
         owners = size // ROWS
         packed = rows_r[g * owners : (g + 1) * owners].reshape(size, WIDE)
-        q = dot_t(spread(packed, d), wq_v[...]).astype(BF16)
-        q_s[g * owners : (g + 1) * owners] = q.reshape(owners, ROWS, cw)
+        whole = spread(packed, d)
+        for h in range(2):
+            q = dot_t(whole, wq_v[h]).astype(BF16)
+            q_s[g * owners : (g + 1) * owners, h] = q.reshape(owners, ROWS, cw)
     send_all(lambda peer: q_s.at[peer], q_r, 1)
-    q_r[me] = q_s[me]
+    q_r[chip] = q_s[chip]
 
     for s in range(3, SLOTS):
         norm_tile(s)
 
     load_k.wait()
     wait_all(q_r, recv_sem.at[1])
-    query = jnp.concatenate([q_r[i].astype(F32) for i in range(n)], axis=1)
+    query = jnp.concatenate([q_r[i, h].astype(F32) for i in range(chips) for h in range(2)], axis=1)
     head_row = lax.broadcasted_iota(jnp.int32, (HEADS, d), 0)
     lane = lax.broadcasted_iota(jnp.int32, (HEADS, d), 1)
     own_head = (lane >= head_row * HEAD_DIM) & (lane < (head_row + 1) * HEAD_DIM)
@@ -242,41 +264,45 @@
     )
     thrice = jnp.concatenate([mixed, mixed, mixed, mixed[0:1]], axis=0)
     for i in range(n):
-        mix_s[i] = thrice[:, i * cw : (i + 1) * cw].astype(BF16)
+        mix_s[i // 2, i % 2] = thrice[:, i * cw : (i + 1) * cw].astype(BF16)
     send_all(lambda peer: mix_s.at[peer], mix_r, 2)
-    mix_r[me] = mix_s[me]
+    mix_r[chip] = mix_s[chip]
 
     load_o.wait()
+    share_o.wait_recv()
     wait_all(mix_r, recv_sem.at[2])
     owners = size // ROWS
     for g in range(groups):
         at = slice(g * owners, (g + 1) * owners)
-        part = dot(mix_r[at].reshape(size, cw), wo_v[...])
+        part = dot(mix_r[at, 0].reshape(size, cw), wo_v[0])
+        part = part + dot(mix_r[at, 1].reshape(size, cw), wo_v[1])
         out_s[at] = fold(part).astype(BF16).reshape(owners, ROWS, WIDE)
     send_all(lambda peer: out_s.at[peer], out_r, 3)
-    out_r[me] = out_s[me]
+    out_r[chip] = out_s[chip]
     wait_all(out_r, recv_sem.at[3])
 
     def total_of(ref):
         acc = ref[0].astype(F32)
-        for i in range(1, n):
+        for i in range(1, chips):
             acc = acc + ref[i].astype(F32)
         return unpack_rows(acc, d)
 
     settled = first + total_of(out_r)
     inner = layer_norm(settled, g_mlp)
-    inner_r[me] = pack_rows(inner).astype(BF16)
-    send_all(lambda peer: inner_r.at[me], inner_r, 4)
+    inner_r[chip] = pack_rows(inner).astype(BF16)
+    send_all(lambda peer: inner_r.at[chip], inner_r, 4)
     load_u.wait()
+    share_u.wait_recv()
     load_d.wait()
+    share_d.wait_recv()
     wait_all(inner_r, recv_sem.at[4])
     for g in range(groups):
         at = slice(g * owners, (g + 1) * owners)
         rows = spread(inner_r[at].reshape(size, WIDE), d)
-        hidden = gelu(dot_t(rows, wu_v[...])).astype(BF16)
-        feed_s[at] = fold(dot(hidden, wd_v[...])).astype(BF16).reshape(owners, ROWS, WIDE)
+        hidden = gelu(dot_t(rows, wu_v[...].reshape(-1, d))).astype(BF16)
+        feed_s[at] = fold(dot(hidden, wd_v[...].reshape(-1, d))).astype(BF16).reshape(owners, ROWS, WIDE)
     send_all(lambda peer: feed_s.at[peer], feed_r, 5)
-    feed_r[me] = feed_s[me]
+    feed_r[chip] = feed_s[chip]
     wait_all(feed_r, recv_sem.at[5])
 
     outcome = settled + total_of(feed_r)
@@ -288,6 +314,8 @@
 
     for phase, ref in enumerate((rows_r, q_s, mix_s, out_s, inner_r, feed_s)):
         wait_all(ref, send_sem.at[phase])
+    for copy in shared:
+        copy.wait_send()
 
 
 def shards(
@@ -301,8 +329,8 @@
     anywhere = pl.BlockSpec(memory_space=pl.ANY)
     vmem = pl.BlockSpec(memory_space=pltpu.VMEM)
     smem = pl.BlockSpec(memory_space=pltpu.SMEM)
-    message = pltpu.VMEM((n, ROWS, WIDE), BF16)
-    narrow = pltpu.VMEM((n, ROWS, cw), BF16)
+    message = pltpu.VMEM((n // 2, ROWS, WIDE), BF16)
+    narrow = pltpu.VMEM((n // 2, 2, ROWS, cw), BF16)
     return pl.pallas_call(
         functools.partial(kernel, n),
         out_shape=jax.ShapeDtypeStruct((counts.shape[0], d), F32),
@@ -313,16 +341,18 @@
             pltpu.VMEM((slots, 16, d), BF16),
             pltpu.VMEM((slots, tok, d), BF16),
             pltpu.VMEM((slots, padded, d), BF16),
-            pltpu.VMEM(w_query.shape, BF16),
+            pltpu.VMEM((2,) + w_query.shape, BF16),
             pltpu.VMEM((d, d), BF16),
             pltpu.VMEM((d, d), BF16),
-            pltpu.VMEM(w_out.shape, BF16),
-            pltpu.VMEM(w_up.shape, BF16),
-            pltpu.VMEM(w_down.shape, BF16),
+            pltpu.VMEM((2,) + w_out.shape, BF16),
+            pltpu.VMEM((2,) + w_up.shape, BF16),
+            pltpu.VMEM((2,) + w_down.shape, BF16),
             message, narrow, narrow, narrow, narrow, message, message, message, message, message,
             pltpu.SemaphoreType.DMA((16,)),
             pltpu.SemaphoreType.DMA((6,)),
             pltpu.SemaphoreType.DMA((6,)),
+            pltpu.SemaphoreType.DMA((4,)),
+            pltpu.SemaphoreType.DMA((4,)),
         ],
         compiler_params=pltpu.CompilerParams(
             collective_id=0, has_side_effects=True, vmem_limit_bytes=60 * 1024 * 1024

time: 53.3 us -> 46.2 us (0.87)
  Pallas kernels: 51 us -> 44 us
    pallas_call x1, Pallas kernels: 51 us -> 44 us  [shards(): pl.pallas_call(functools.partial(kernel, n), out_shape=jax.ShapeDtypeStru...]
where the time goes in v3:
time: 46.2 us; the launch traced here: 46 us
  Pallas kernels  44 us (95%)
  local copies, waits for them, and re-layouts  1.28 us (3%)
  between operations  0.66 us (1%)
    pallas_call x1, Pallas kernels, shards(): pl.pallas_call(functools.partial(kernel, n), out_shape=jax.ShapeDtypeStru...  44 us
    unnamed x1, local copies, waits for them, and re-layouts  1.28 us

profile of v3, /device:TPU:0, one launch (start us, length us, event | category | flops | bytes accessed | tf_op | source)
XLA Modules:
  0.0 46.0 jit_solution(12429138832089025080)
XLA Ops:
  0.7 44.0 %shard_map.109 = f32[1,1280]{1,0:T(1,128)} custom-call(bf16[5,257,1280]{2,1,0:T(8,128)(2,1)} %tiles.1, s32[1]{0:T(128)S(6)} %copy.13.counts, bf16[80,1280]{1,0:T(8,128)(2,1)} %bitcast.3, bf16[1280,2560]{1,0:T(8,128)(2,1)} %w_keyval.1, bf16[80,1280]{1,0:T(8,128)(2,1)} %w_out.1, bf16[320,1280]{1,0:T(8,128)(2,1)} %bitcast.2, bf16[320,1280]{1,0:T(8,128)(2,1)} %w_down.1, ...), custom_call_target="tpu_custom_call" | custom-call | tf_op jit(solution)/shard_map/pallas_call | solution.py:334
  44.7 1.3 %copy.14 = f32[1,1280]{1,0:T(1,128)} copy(f32[1,1280]{1,0:T(1,128)} %shard_map.109) | data formatting | bytes 10240

commit v4 on v3

--- a/solution.py
+++ b/solution.py
@@ -153,7 +153,8 @@
 
     def send_all(src_at, dst, phase):
         def body(k, _):
-            peer = lax.rem(chip + k, chips)
+            away = 1 + lax.rem(k + chips // 2 - 2, chips - 1)
+            peer = lax.rem(chip + away, chips)
             pltpu.make_async_remote_copy(
                 src_ref=src_at(peer),
                 dst_ref=dst.at[chip],
@@ -194,6 +195,8 @@
         shared.append(copy)
     share_q, share_o, share_u, share_d = shared
 
+    whole = tok // 256 * 256
+
     def norm_tile(s):
         load_tiles[s].wait()
 
@@ -202,9 +205,7 @@
             normed_v[s, at, :] = layer_norm(tiles_v[s, at, :].astype(F32), g_attn).astype(BF16)
             return 0
 
-        lax.fori_loop(0, tok // 32, body, 0, unroll=2)
-        whole = tok // 32 * 32
-        rest = tok - whole
+        lax.fori_loop(0, whole // 32, body, 0, unroll=2)
         tail = layer_norm(tiles_v[s, whole:tok, :].astype(F32), g_attn)
         tail = jnp.concatenate(
             [tail, jnp.zeros((normed_v.shape[1] - tok, d), F32)], axis=0
@@ -220,9 +221,9 @@
     for g in range(groups):
         owners = size // ROWS
         packed = rows_r[g * owners : (g + 1) * owners].reshape(size, WIDE)
-        whole = spread(packed, d)
+        each = spread(packed, d)
         for h in range(2):
-            q = dot_t(whole, wq_v[h]).astype(BF16)
+            q = dot_t(each, wq_v[h]).astype(BF16)
             q_s[g * owners : (g + 1) * owners, h] = q.reshape(owners, ROWS, cw)
     send_all(lambda peer: q_s.at[peer], q_r, 1)
     q_r[chip] = q_s[chip]
@@ -240,15 +241,34 @@
         [jnp.where(own_head, query[s : s + 1], 0.0).astype(BF16) for s in range(SLOTS)], axis=0
     )
     keyed = dot_t(apart, wk_v[...]).astype(BF16)
-    padded = normed_v.shape[1]
-    real = lax.broadcasted_iota(jnp.int32, (HEADS, padded), 1) < tok
+    parts = [keyed[s * HEADS : (s + 1) * HEADS] for s in range(SLOTS)]
+    scores = jnp.concatenate([dot_t(parts[s], normed_v[s, :whole, :]) for s in range(SLOTS)], axis=0)
+    wide_keyed = keyed.astype(F32)
+    extra = []
+    for t in range(whole, tok):
+        rows = [
+            jnp.broadcast_to(normed_v[s, t : t + 1, :].astype(F32), (HEADS, d)) for s in range(SLOTS)
+        ]
+        extra.append(
+            (rows, jnp.sum(wide_keyed * jnp.concatenate(rows, axis=0), axis=-1, keepdims=True))
+        )
+    scale = 1.0 / math.sqrt(HEAD_DIM)
+    scores = scores * scale
+    peak = jnp.max(scores, axis=-1, keepdims=True)
+    for _, score in extra:
+        peak = jnp.maximum(peak, score * scale)
+    weights = jnp.exp(scores - peak)
+    last = [jnp.exp(score * scale - peak) for _, score in extra]
+    norm = 1.0 / (jnp.sum(weights, axis=-1, keepdims=True) + sum(last))
+    weights = (weights * norm).astype(BF16)
+    last = [(w * norm).astype(BF16).astype(F32) for w in last]
     context = []
     for s in range(SLOTS):
-        scores = dot_t(keyed[s * HEADS : (s + 1) * HEADS], normed_v[s]) / math.sqrt(HEAD_DIM)
-        scores = jnp.where(real, scores, -jnp.inf)
-        weights = jnp.exp(scores - jnp.max(scores, axis=-1, keepdims=True))
-        weights = weights / jnp.sum(weights, axis=-1, keepdims=True)
-        context.append(dot(weights.astype(BF16), normed_v[s]).astype(BF16))
+        at = slice(s * HEADS, (s + 1) * HEADS)
+        mean = dot(weights[at], normed_v[s, :whole, :])
+        for (rows, _), w in zip(extra, last):
+            mean = mean + w[at] * rows[s]
+        context.append(mean.astype(BF16))
     load_v.wait()
     valued = dot(jnp.concatenate(context, axis=0), wv_v[...])
     mixed = jnp.concatenate(

time: 46.2 us -> 44.2 us (0.957)
  Pallas kernels: 44 us -> 42 us
    pallas_call x1, Pallas kernels: 44 us -> 42 us  [shards(): pl.pallas_call(functools.partial(kernel, n), out_shape=jax.ShapeDtypeStru...]
where the time goes in v4:
time: 44.2 us; the launch traced here: 44 us
  Pallas kernels  42 us (95%)
  local copies, waits for them, and re-layouts  1.28 us (3%)
  between operations  0.66 us (1%)
    pallas_call x1, Pallas kernels, shards(): pl.pallas_call(functools.partial(kernel, n), out_shape=jax.ShapeDtypeStru...  42 us
    unnamed x1, local copies, waits for them, and re-layouts  1.28 us

profile of v4, /device:TPU:0, one launch (start us, length us, event | category | flops | bytes accessed | tf_op | source)
XLA Modules:
  0.0 44.0 jit_solution(16430080769702921188)
XLA Ops:
  0.7 42.0 %shard_map.109 = f32[1,1280]{1,0:T(1,128)} custom-call(bf16[5,257,1280]{2,1,0:T(8,128)(2,1)} %tiles.1, s32[1]{0:T(128)S(6)} %copy.13.counts, bf16[80,1280]{1,0:T(8,128)(2,1)} %bitcast.3, bf16[1280,2560]{1,0:T(8,128)(2,1)} %w_keyval.1, bf16[80,1280]{1,0:T(8,128)(2,1)} %w_out.1, bf16[320,1280]{1,0:T(8,128)(2,1)} %bitcast.2, bf16[320,1280]{1,0:T(8,128)(2,1)} %w_down.1, ...), custom_call_target="tpu_custom_call" | custom-call | tf_op jit(solution)/shard_map/pallas_call | solution.py:354
  42.7 1.3 %copy.14 = f32[1,1280]{1,0:T(1,128)} copy(f32[1,1280]{1,0:T(1,128)} %shard_map.109) | data formatting | bytes 10240

commit v5 on v4

--- a/solution.py
+++ b/solution.py
@@ -120,6 +120,16 @@
     groups = max(total // GROUP, 1)
     size = total // groups
 
+    barrier = pltpu.get_barrier_semaphore()
+
+    def greet(k, _):
+        peer = lax.rem(chip + k, chips) * 2 + core
+        pl.semaphore_signal(barrier, inc=1, device_id={"dp": peer}, device_id_type=MESH)
+        return 0
+
+    pl.semaphore_signal(barrier, inc=1, device_id={"dp": sibling}, device_id_type=MESH)
+    lax.fori_loop(1, chips, greet, 0)
+
     loads = []
 
     def load(src, dst):
@@ -141,20 +151,9 @@
     load_u = load(w_up, wu_v.at[core])
     load_d = load(w_down, wd_v.at[core])
 
-    barrier = pltpu.get_barrier_semaphore()
-
-    def greet(k, _):
-        peer = lax.rem(chip + k, chips) * 2 + core
-        pl.semaphore_signal(barrier, inc=1, device_id={"dp": peer}, device_id_type=MESH)
-        return 0
-
-    pl.semaphore_signal(barrier, inc=1, device_id={"dp": sibling}, device_id_type=MESH)
-    lax.fori_loop(1, chips, greet, 0)
-
     def send_all(src_at, dst, phase):
         def body(k, _):
-            away = 1 + lax.rem(k + chips // 2 - 2, chips - 1)
-            peer = lax.rem(chip + away, chips)
+            peer = lax.rem(chip + k, chips)
             pltpu.make_async_remote_copy(
                 src_ref=src_at(peer),
                 dst_ref=dst.at[chip],
@@ -212,7 +211,7 @@
         )
         normed_v[s, whole:, :] = tail.astype(BF16)
 
-    for s in range(3):
+    for s in range(SLOTS):
         norm_tile(s)
 
     load_q.wait()
@@ -227,9 +226,6 @@
             q_s[g * owners : (g + 1) * owners, h] = q.reshape(owners, ROWS, cw)
     send_all(lambda peer: q_s.at[peer], q_r, 1)
     q_r[chip] = q_s[chip]
-
-    for s in range(3, SLOTS):
-        norm_tile(s)
 
     load_k.wait()
     wait_all(q_r, recv_sem.at[1])

time: 44.2 us -> 42.9 us (0.971)
  Pallas kernels: 42 us -> 40.7 us
    pallas_call x1, Pallas kernels: 42 us -> 40.7 us  [shards(): pl.pallas_call(functools.partial(kernel, n), out_shape=jax.ShapeDtypeStru...]
where the time goes in v5:
time: 42.9 us; the launch traced here: 42.7 us
  Pallas kernels  40.7 us (95%)
  local copies, waits for them, and re-layouts  1.28 us (3%)
  between operations  0.66 us (2%)
    pallas_call x1, Pallas kernels, shards(): pl.pallas_call(functools.partial(kernel, n), out_shape=jax.ShapeDtypeStru...  40.7 us
    unnamed x1, local copies, waits for them, and re-layouts  1.28 us

profile of v5, /device:TPU:0, one launch (start us, length us, event | category | flops | bytes accessed | tf_op | source)
XLA Modules:
  0.0 42.7 jit_solution(6511652524765337249)
XLA Ops:
  0.7 40.7 %shard_map.109 = f32[1,1280]{1,0:T(1,128)} custom-call(bf16[5,257,1280]{2,1,0:T(8,128)(2,1)} %tiles.1, s32[1]{0:T(128)S(6)} %copy.13.counts, bf16[80,1280]{1,0:T(8,128)(2,1)} %bitcast.3, bf16[1280,2560]{1,0:T(8,128)(2,1)} %w_keyval.1, bf16[80,1280]{1,0:T(8,128)(2,1)} %w_out.1, bf16[320,1280]{1,0:T(8,128)(2,1)} %bitcast.2, bf16[320,1280]{1,0:T(8,128)(2,1)} %w_down.1, ...), custom_call_target="tpu_custom_call" | custom-call | tf_op jit(solution)/shard_map/pallas_call | solution.py:350
  41.4 1.3 %copy.14 = f32[1,1280]{1,0:T(1,128)} copy(f32[1,1280]{1,0:T(1,128)} %shard_map.109) | data formatting | bytes 10240

commit v6 on v5

--- a/solution.py
+++ b/solution.py
@@ -13,6 +13,8 @@
 SLOTS = 5
 ROWS = 16
 WIDE = 512
+HALF = 256
+PARTS = ((0, 3), (3, 5))
 GROUP = 256
 
 epsilon = 1e-05
@@ -64,41 +66,52 @@
     return lax.dot_general(a, b, (((1,), (1,)), ((), ())), preferred_element_type=F32)
 
 
-def pack_rows(x):
-    d = x.shape[1]
-    last = jnp.concatenate([x[:, 2 * WIDE :], jnp.zeros((SLOTS, 3 * WIDE - d), F32)], axis=1)
+def pack_rows(x, wide):
+    slots, d = x.shape
+    blocks = -(-d // wide)
+    pieces = [x[:, c * wide : (c + 1) * wide] for c in range(blocks)]
+    if blocks * wide > d:
+        short = jnp.zeros((slots, blocks * wide - d), F32)
+        pieces[-1] = jnp.concatenate([pieces[-1], short], axis=1)
+    pieces.append(jnp.zeros((ROWS - slots * blocks, wide), F32))
+    return jnp.concatenate(pieces, axis=0)
+
+
+def unpack_rows(p, slots, d):
+    wide = p.shape[1]
+    blocks = -(-d // wide)
     return jnp.concatenate(
-        [x[:, :WIDE], x[:, WIDE : 2 * WIDE], last, jnp.zeros((1, WIDE), F32)], axis=0
+        [p[c * slots : (c + 1) * slots, : min(wide, d - c * wide)] for c in range(blocks)], axis=1
     )
 
 
-def unpack_rows(p, d):
-    return jnp.concatenate(
-        [p[0:SLOTS], p[SLOTS : 2 * SLOTS], p[2 * SLOTS : 3 * SLOTS, : d - 2 * WIDE]], axis=1
-    )
-
-
-def spread(packed, d):
-    size = packed.shape[0]
+def pick(size, slots, offset):
     r = lax.broadcasted_iota(jnp.int32, (size, size), 0)
     c = lax.broadcasted_iota(jnp.int32, (size, size), 1)
-    same = (r >> 4) == (c >> 4)
     rm = r & 15
-    slot = rm - jnp.where(rm >= 5, 5, 0) - jnp.where(rm >= 10, 5, 0) - jnp.where(rm >= 15, 5, 0)
-    cm = c & 15
+    slot = rm
+    for k in range(slots, ROWS, slots):
+        slot = slot - jnp.where(rm >= k, slots, 0)
+    return jnp.where(((r >> 4) == (c >> 4)) & ((c & 15) == slot + offset), 1.0, 0.0).astype(BF16)
+
+
+def spread(packed, slots, d):
+    size, wide = packed.shape
     out = []
-    for k in range(3):
-        pick = jnp.where(same & (cm == slot + 5 * k), 1.0, 0.0).astype(BF16)
-        src = packed if k < 2 else packed[:, : d - 2 * WIDE]
-        out.append(dot(pick, src).astype(BF16))
+    for c in range(-(-d // wide)):
+        src = packed[:, : min(wide, d - c * wide)]
+        out.append(dot(pick(size, slots, c * slots), src).astype(BF16))
     return jnp.concatenate(out, axis=1)
 
 
-def fold(y):
+def fold(y, slots, wide):
     size, d = y.shape
-    rm = lax.broadcasted_iota(jnp.int32, (size, WIDE), 0) & 15
-    last = jnp.concatenate([y[:, 2 * WIDE :], jnp.zeros((size, 3 * WIDE - d), F32)], axis=1)
-    return jnp.where(rm < 5, y[:, :WIDE], jnp.where(rm < 10, y[:, WIDE : 2 * WIDE], last))
+    blocks = d // wide
+    rm = lax.broadcasted_iota(jnp.int32, (size, wide), 0) & 15
+    out = y[:, (blocks - 1) * wide :]
+    for c in range(blocks - 2, -1, -1):
+        out = jnp.where(rm < (c + 1) * slots, y[:, c * wide : (c + 1) * wide], out)
+    return out
 
 
 def kernel(
@@ -176,7 +189,7 @@
 
     load_first.wait()
     first = jnp.concatenate([first_v[s, 0:1, :].astype(F32) for s in range(SLOTS)], axis=0)
-    rows_r[chip] = pack_rows(layer_norm(first, g_attn)).astype(BF16)
+    rows_r[chip] = pack_rows(layer_norm(first, g_attn), WIDE).astype(BF16)
     pl.semaphore_wait(barrier, chips)
     send_all(lambda peer: rows_r.at[chip], rows_r, 0)
 
@@ -220,7 +233,7 @@
     for g in range(groups):
         owners = size // ROWS
         packed = rows_r[g * owners : (g + 1) * owners].reshape(size, WIDE)
-        each = spread(packed, d)
+        each = spread(packed, SLOTS, d)
         for h in range(2):
             q = dot_t(each, wq_v[h]).astype(BF16)
             q_s[g * owners : (g + 1) * owners, h] = q.reshape(owners, ROWS, cw)
@@ -288,47 +301,61 @@
     share_o.wait_recv()
     wait_all(mix_r, recv_sem.at[2])
     owners = size // ROWS
-    for g in range(groups):
-        at = slice(g * owners, (g + 1) * owners)
-        part = dot(mix_r[at, 0].reshape(size, cw), wo_v[0])
-        part = part + dot(mix_r[at, 1].reshape(size, cw), wo_v[1])
-        out_s[at] = fold(part).astype(BF16).reshape(owners, ROWS, WIDE)
-    send_all(lambda peer: out_s.at[peer], out_r, 3)
-    out_r[chip] = out_s[chip]
-    wait_all(out_r, recv_sem.at[3])
-
-    def total_of(ref):
-        acc = ref[0].astype(F32)
+    spans = [slice(g * owners, (g + 1) * owners) for g in range(groups)]
+    for h, (low, high) in enumerate(PARTS):
+        slots = high - low
+        for at in spans:
+            moved = pick(size, slots, low)
+            part = 0.0
+            for c in range(2):
+                column = dot(moved, mix_r[at, c].reshape(size, cw)).astype(BF16)
+                part = part + dot(column, wo_v[c])
+            out_s[h, at] = fold(part, slots, HALF).astype(BF16).reshape(owners, ROWS, HALF)
+        send_all(lambda peer: out_s.at[h, peer], out_r.at[h], 3 + h)
+        out_r[h, chip] = out_s[h, chip]
+
+    def total_of(ref, h, slots):
+        acc = ref[h, 0].astype(F32)
         for i in range(1, chips):
-            acc = acc + ref[i].astype(F32)
-        return unpack_rows(acc, d)
-
-    settled = first + total_of(out_r)
-    inner = layer_norm(settled, g_mlp)
-    inner_r[chip] = pack_rows(inner).astype(BF16)
-    send_all(lambda peer: inner_r.at[chip], inner_r, 4)
+            acc = acc + ref[h, i].astype(F32)
+        return unpack_rows(acc, slots, d)
+
+    settled = []
+    for h, (low, high) in enumerate(PARTS):
+        wait_all(out_r.at[h], recv_sem.at[3 + h])
+        settled.append(first[low:high] + total_of(out_r, h, high - low))
+        inner_r[h, chip] = pack_rows(layer_norm(settled[h], g_mlp), HALF).astype(BF16)
+        send_all(lambda peer: inner_r.at[h, chip], inner_r.at[h], 5 + h)
+
     load_u.wait()
     share_u.wait_recv()
     load_d.wait()
     share_d.wait_recv()
-    wait_all(inner_r, recv_sem.at[4])
-    for g in range(groups):
-        at = slice(g * owners, (g + 1) * owners)
-        rows = spread(inner_r[at].reshape(size, WIDE), d)
-        hidden = gelu(dot_t(rows, wu_v[...].reshape(-1, d))).astype(BF16)
-        feed_s[at] = fold(dot(hidden, wd_v[...].reshape(-1, d))).astype(BF16).reshape(owners, ROWS, WIDE)
-    send_all(lambda peer: feed_s.at[peer], feed_r, 5)
-    feed_r[chip] = feed_s[chip]
-    wait_all(feed_r, recv_sem.at[5])
-
-    outcome = settled + total_of(feed_r)
-    final = layer_norm(outcome, g_post) + b_post
+    for h, (low, high) in enumerate(PARTS):
+        slots = high - low
+        wait_all(inner_r.at[h], recv_sem.at[5 + h])
+        for at in spans:
+            rows = spread(inner_r[h, at].reshape(size, HALF), slots, d)
+            hidden = gelu(dot_t(rows, wu_v[...].reshape(-1, d))).astype(BF16)
+            feed = dot(hidden, wd_v[...].reshape(-1, d))
+            feed_s[h, at] = fold(feed, slots, HALF).astype(BF16).reshape(owners, ROWS, HALF)
+        send_all(lambda peer: feed_s.at[h, peer], feed_r.at[h], 7 + h)
+        feed_r[h, chip] = feed_s[h, chip]
+
     count = counts[0]
-    present = lax.broadcasted_iota(jnp.int32, (SLOTS, d), 0) < count
-    summed = jnp.sum(jnp.where(present, final, 0.0), axis=0, keepdims=True)
+    summed = jnp.zeros((1, d), F32)
+    for h, (low, high) in enumerate(PARTS):
+        wait_all(feed_r.at[h], recv_sem.at[7 + h])
+        outcome = settled[h] + total_of(feed_r, h, high - low)
+        final = layer_norm(outcome, g_post) + b_post
+        present = lax.broadcasted_iota(jnp.int32, (high - low, d), 0) + low < count
+        summed = summed + jnp.sum(jnp.where(present, final, 0.0), axis=0, keepdims=True)
     out[...] = summed / jnp.full((1, d), count, jnp.int32).astype(F32)
 
-    for phase, ref in enumerate((rows_r, q_s, mix_s, out_s, inner_r, feed_s)):
+    sent = [rows_r, q_s, mix_s]
+    for ref in (out_s, inner_r, feed_s):
+        sent += [ref.at[0], ref.at[1]]
+    for phase, ref in enumerate(sent):
         wait_all(ref, send_sem.at[phase])
     for copy in shared:
         copy.wait_send()
@@ -346,6 +373,7 @@
     vmem = pl.BlockSpec(memory_space=pltpu.VMEM)
     smem = pl.BlockSpec(memory_space=pltpu.SMEM)
     message = pltpu.VMEM((n // 2, ROWS, WIDE), BF16)
+    halved = pltpu.VMEM((2, n // 2, ROWS, HALF), BF16)
     narrow = pltpu.VMEM((n // 2, 2, ROWS, cw), BF16)
     return pl.pallas_call(
         functools.partial(kernel, n),
@@ -363,10 +391,10 @@
             pltpu.VMEM((2,) + w_out.shape, BF16),
             pltpu.VMEM((2,) + w_up.shape, BF16),
             pltpu.VMEM((2,) + w_down.shape, BF16),
-            message, narrow, narrow, narrow, narrow, message, message, message, message, message,
+            message, narrow, narrow, narrow, narrow, halved, halved, halved, halved, halved,
             pltpu.SemaphoreType.DMA((16,)),
-            pltpu.SemaphoreType.DMA((6,)),
-            pltpu.SemaphoreType.DMA((6,)),
+            pltpu.SemaphoreType.DMA((9,)),
+            pltpu.SemaphoreType.DMA((9,)),
             pltpu.SemaphoreType.DMA((4,)),
             pltpu.SemaphoreType.DMA((4,)),
         ],

time: 42.9 us -> 42.8 us (level)
  no operation moved by 1% of the time
where the time goes in v6:
time: 42.8 us; the launch traced here: 42.6 us
  Pallas kernels  40.7 us (95%)
  local copies, waits for them, and re-layouts  1.28 us (3%)
  between operations  0.66 us (2%)
    pallas_call x1, Pallas kernels, shards(): pl.pallas_call(functools.partial(kernel, n), out_shape=jax.ShapeDtypeStru...  40.7 us
    unnamed x1, local copies, waits for them, and re-layouts  1.28 us

profile of v6, /device:TPU:0, one launch (start us, length us, event | category | flops | bytes accessed | tf_op | source)
XLA Modules:
  0.0 42.6 jit_solution(3388939798761585835)
XLA Ops:
  0.7 40.7 %shard_map.109 = f32[1,1280]{1,0:T(1,128)} custom-call(bf16[5,257,1280]{2,1,0:T(8,128)(2,1)} %tiles.1, s32[1]{0:T(128)S(6)} %copy.13.counts, bf16[80,1280]{1,0:T(8,128)(2,1)} %bitcast.3, bf16[1280,2560]{1,0:T(8,128)(2,1)} %w_keyval.1, bf16[80,1280]{1,0:T(8,128)(2,1)} %w_out.1, bf16[320,1280]{1,0:T(8,128)(2,1)} %bitcast.2, bf16[320,1280]{1,0:T(8,128)(2,1)} %w_down.1, ...), custom_call_target="tpu_custom_call" | custom-call | tf_op jit(solution)/shard_map/pallas_call | solution.py:378
  41.3 1.3 %copy.14 = f32[1,1280]{1,0:T(1,128)} copy(f32[1,1280]{1,0:T(1,128)} %shard_map.109) | data formatting | bytes 10240

commit v7 on v6

--- a/solution.py
+++ b/solution.py
@@ -234,15 +234,17 @@
         owners = size // ROWS
         packed = rows_r[g * owners : (g + 1) * owners].reshape(size, WIDE)
         each = spread(packed, SLOTS, d)
-        for h in range(2):
-            q = dot_t(each, wq_v[h]).astype(BF16)
-            q_s[g * owners : (g + 1) * owners, h] = q.reshape(owners, ROWS, cw)
+        upper = (lax.broadcasted_iota(jnp.int32, (size, cw), 0) & 15) < SLOTS
+        q = jnp.where(upper, dot_t(each, wq_v[0]), dot_t(each, wq_v[1])).astype(BF16)
+        q_s[g * owners : (g + 1) * owners] = q.reshape(owners, ROWS, cw)
     send_all(lambda peer: q_s.at[peer], q_r, 1)
     q_r[chip] = q_s[chip]
 
     load_k.wait()
     wait_all(q_r, recv_sem.at[1])
-    query = jnp.concatenate([q_r[i, h].astype(F32) for i in range(chips) for h in range(2)], axis=1)
+    query = jnp.concatenate([
+            q_r[i].astype(F32)[h * SLOTS : (h + 1) * SLOTS] for i in range(chips) for h in range(2)
+        ], axis=1)
     head_row = lax.broadcasted_iota(jnp.int32, (HEADS, d), 0)
     lane = lax.broadcasted_iota(jnp.int32, (HEADS, d), 1)
     own_head = (lane >= head_row * HEAD_DIM) & (lane < (head_row + 1) * HEAD_DIM)
@@ -291,9 +293,10 @@
         ],
         axis=0,
     )
-    thrice = jnp.concatenate([mixed, mixed, mixed, mixed[0:1]], axis=0)
-    for i in range(n):
-        mix_s[i // 2, i % 2] = thrice[:, i * cw : (i + 1) * cw].astype(BF16)
+    spare = jnp.zeros((ROWS - 2 * SLOTS, cw), F32)
+    for i in range(chips):
+        pair = [mixed[:, c * cw : (c + 1) * cw] for c in (2 * i, 2 * i + 1)]
+        mix_s[i] = jnp.concatenate(pair + [spare], axis=0).astype(BF16)
     send_all(lambda peer: mix_s.at[peer], mix_r, 2)
     mix_r[chip] = mix_s[chip]
 
@@ -305,10 +308,10 @@
     for h, (low, high) in enumerate(PARTS):
         slots = high - low
         for at in spans:
-            moved = pick(size, slots, low)
             part = 0.0
             for c in range(2):
-                column = dot(moved, mix_r[at, c].reshape(size, cw)).astype(BF16)
+                moved = pick(size, slots, low + c * SLOTS)
+                column = dot(moved, mix_r[at].reshape(size, cw)).astype(BF16)
                 part = part + dot(column, wo_v[c])
             out_s[h, at] = fold(part, slots, HALF).astype(BF16).reshape(owners, ROWS, HALF)
         send_all(lambda peer: out_s.at[h, peer], out_r.at[h], 3 + h)
@@ -374,7 +377,7 @@
     smem = pl.BlockSpec(memory_space=pltpu.SMEM)
     message = pltpu.VMEM((n // 2, ROWS, WIDE), BF16)
     halved = pltpu.VMEM((2, n // 2, ROWS, HALF), BF16)
-    narrow = pltpu.VMEM((n // 2, 2, ROWS, cw), BF16)
+    narrow = pltpu.VMEM((n // 2, ROWS, cw), BF16)
     return pl.pallas_call(
         functools.partial(kernel, n),
         out_shape=jax.ShapeDtypeStruct((counts.shape[0], d), F32),

time: 42.8 us -> 42.6 us (level)
  no operation moved by 1% of the time
where the time goes in v7:
time: 42.6 us; the launch traced here: 42.3 us
  Pallas kernels  40.4 us (95%)
  local copies, waits for them, and re-layouts  1.28 us (3%)
  between operations  0.66 us (2%)
    pallas_call x1, Pallas kernels, shards(): pl.pallas_call(functools.partial(kernel, n), out_shape=jax.ShapeDtypeStru...  40.4 us
    unnamed x1, local copies, waits for them, and re-layouts  1.28 us

profile of v7, /device:TPU:0, one launch (start us, length us, event | category | flops | bytes accessed | tf_op | source)
XLA Modules:
  0.0 42.3 jit_solution(10036436787299384208)
XLA Ops:
  0.7 40.4 %shard_map.109 = f32[1,1280]{1,0:T(1,128)} custom-call(bf16[5,257,1280]{2,1,0:T(8,128)(2,1)} %tiles.1, s32[1]{0:T(128)S(6)} %copy.13.counts, bf16[80,1280]{1,0:T(8,128)(2,1)} %bitcast.3, bf16[1280,2560]{1,0:T(8,128)(2,1)} %w_keyval.1, bf16[80,1280]{1,0:T(8,128)(2,1)} %w_out.1, bf16[320,1280]{1,0:T(8,128)(2,1)} %bitcast.2, bf16[320,1280]{1,0:T(8,128)(2,1)} %w_down.1, ...), custom_call_target="tpu_custom_call" | custom-call | tf_op jit(solution)/shard_map/pallas_call | solution.py:381
  41.1 1.3 %copy.14 = f32[1,1280]{1,0:T(1,128)} copy(f32[1,1280]{1,0:T(1,128)} %shard_map.109) | data formatting | bytes 10240
